TPU v7x, 32 devices: a whole 2x2x4 slice. The times are simulated.
32 devices in a mesh: freq: 16 (over z, x, core), space: 2 (over y).
Axes of the slice: x: 2, y: 2, z: 4, core: 2. Of those that a mesh axis runs over, the one named last changes fastest.
Arguments:
- series: bfloat16 [2048, 32768], P('freq', 'space')
- starts: int32 [7], replicated, may hold values from 0 to 1536, as said below
- freqs: int32 [16], replicated, may hold values from 0 to 511, as said below
- alpha: int32 [1], replicated, may hold values from 1 to 63
Outputs:
- spectra: bfloat16 [16, 2, 7, 32768], P('freq', None, None, 'space')
- gram: float32 [16, 2, 63, 63], P('freq')
Inputs may be any that keep to these rules, and one draw needn't show every extreme that they name: `starts`: increasing; the first is 0, the last 1536; consecutive ones lie 512 / 4 to 384 apart. `freqs`: 16 distinct bins, 0 and 511 among them.
All inputs are finite; a program needn't handle non-finite values.
Results may differ from a plain program's by a relative error of at most 0.005.
Values may be sent and summed in bfloat16 or wider, within the bound.
A program may use at most 64 MiB of HBM per device.

v0:
```python
import math

import jax
import jax.numpy as jnp
from jax import lax
from jax.sharding import PartitionSpec as P

NFFT = 512
NBLK = 7
HALF = 4
SHIFTS = 9


def transform_table(freqs, alpha):
    sample_index = jnp.arange(NFFT, dtype=jnp.int32)
    shift_index = jnp.arange(SHIFTS, dtype=jnp.int32) - HALF
    freq_bins = jnp.mod(freqs[:, None] + shift_index[None, :] * alpha[0], NFFT)
    phase_steps = jnp.mod(freq_bins[:, :, None] * sample_index[None, None, :], NFFT)
    phase = phase_steps.astype(jnp.float32) * (2.0 * math.pi / NFFT)
    sample_float = sample_index.astype(jnp.float32)
    window_shape = 0.5 - 0.5 * jnp.cos(sample_float * (2.0 * math.pi / NFFT))
    window_scale = window_shape / jnp.sqrt(jnp.sum(window_shape * window_shape))
    real_part = window_scale * jnp.cos(phase)
    imag_part = -(window_scale * jnp.sin(phase))
    return jnp.stack([real_part, imag_part], axis=1).astype(jnp.bfloat16)


def split_quadrants(products, order):
    real_gram = products[..., :order, :order] + products[..., order:, order:]
    imag_gram = products[..., :order, order:] - products[..., order:, :order]
    return jnp.stack([real_gram, imag_gram], axis=-3)


def per_device(series, starts, freqs, alpha):
    slab_cells = series.shape[1]
    total_cells = slab_cells * lax.axis_size("space")
    nfreq = freqs.shape[0]
    order = SHIFTS * NBLK
    local_rows = lax.all_to_all(series, "freq", split_axis=1, concat_axis=0, tiled=True)
    local_cells = local_rows.shape[1]
    flat_table = transform_table(freqs, alpha).reshape(nfreq * 2 * SHIFTS, NFFT)
    blocks = []
    for block in range(NBLK):
        block_rows = lax.dynamic_slice_in_dim(local_rows, starts[block], NFFT, 0)
        spec_block = jnp.dot(flat_table, block_rows, preferred_element_type=jnp.float32)
        blocks.append(spec_block.astype(jnp.bfloat16).reshape(nfreq, 2, SHIFTS, local_cells))
    blockspec = jnp.stack(blocks, axis=3)
    received = lax.all_to_all(blockspec, "freq", split_axis=0, concat_axis=4, tiled=True)
    stacked = received.reshape(2 * order, slab_cells)
    products = lax.dot_general(
        stacked, stacked, (((1,), (1,)), ((), ())), preferred_element_type=jnp.float32
    )
    gram_part = split_quadrants(products, order)[None]
    own_spectra = received[:, :, HALF]
    gram = lax.psum(gram_part, "space") / total_cells
    return (own_spectra, gram)


def solution(mesh):
    placed = (P("freq", "space"), P(), P(), P())
    return jax.shard_map(
        per_device,
        mesh=mesh,
        in_specs=placed,
        out_specs=(P("freq", None, None, "space"), P("freq", None, None, None)),
        check_vma=False,
    )
```

profile of v0, /device:TPU:0, one launch (start us, length us, event | category | flops | bytes accessed | tf_op | source)
XLA Modules:
  0.0 275.9 jit_solution(13323514239728539660)
XLA Ops:
  0.6 6.4 %copy.22 = bf16[128,16384]{0,1:T(8,128)(2,1)} copy(bf16[128,16384]{1,0:T(8,128)(2,1)} %param.4) | data formatting | bytes 8388608 | tf_op args[0]
  7.1 7.5 %all-to-all-start = ((bf16[128,16,1024]{0,2,1:T(8,128)(2,1)}), bf16[128,16,1024]{0,2,1:T(8,128)(2,1)}, u32[]{:S(2)}, u32[]{:S(2)}) async-start(bf16[128,16,1024]{0,2,1:T(8,128)(2,1)} %bitcast.48), calls=%async_computation | async-start | bytes 8388608 | tf_op jit(solution)/shard_map/all_to_all | solution.py:39
  26.3 1.4 multiply_convert_fusion
  32.5 59.8 %all-to-all-done = bf16[128,16,1024]{0,2,1:T(8,128)(2,1)} async-done(((bf16[128,16,1024]{0,2,1:T(8,128)(2,1)}), bf16[128,16,1024]{0,2,1:T(8,128)(2,1)}, u32[]{:S(2)}, u32[]{:S(2)}) %all-to-all-start) | async-done | bytes 4194336 | tf_op jit(solution)/shard_map/all_to_all | solution.py:39
  92.3 6.4 %copy.23 = bf16[16,128,1024]{2,1,0:T(8,128)(2,1)} copy(bf16[16,128,1024]{1,2,0:T(8,128)(2,1)} %bitcast.2) | data formatting | bytes 8388608 | tf_op jit(solution)/shard_map/all_to_all | solution.py:39
  98.7 1.7 convolution_convert_fusion.6
  100.7 1.1 constant_dynamic-update-slice_fusion.6
  101.7 1.7 convolution_convert_fusion.5
  103.7 1.7 convolution_convert_fusion.4
  105.7 2.6 convolution_convert_fusion.3
  108.3 1.3 stack_reshape.24
  109.6 2.6 convolution_convert_fusion.2
  112.2 2.2 stack_reshape.25
  114.4 2.6 convolution_convert_fusion.1
  116.9 2.2 stack_reshape.26
  119.1 2.6 convolution_convert_fusion
  121.7 2.2 stack_reshape.27
  123.9 1.1 constant_dynamic-update-slice_fusion.5
  125.0 1.1 constant_dynamic-update-slice_fusion.4
  126.1 1.1 constant_dynamic-update-slice_fusion.3
  127.1 1.1 constant_dynamic-update-slice_fusion.2
  128.2 1.1 constant_dynamic-update-slice_fusion.1
  129.3 1.1 constant_dynamic-update-slice_fusion
  130.3 9.8 %copy.24 = bf16[16,2,9,7,1024]{4,1,3,2,0:T(2,128)(2,1)} copy(bf16[16,2,9,7,1024]{4,2,1,0,3:T(8,128)(2,1)} %constant_dynamic-update-slice_fusion) | data formatting | bytes 8257536 | tf_op jit(solution)/shard_map/stack | solution.py:47
  140.2 110.8 %all_to_all.37 = bf16[16,2,9,7,1024]{4,1,3,2,0:T(2,128)(2,1)S(1)} all-to-all(bf16[16,2,9,7,1024]{4,1,3,2,0:T(2,128)(2,1)} %copy.24), channel_id=1, replica_groups=mesh['freq'=16,'space'=2] {'freq'}, dimensions={0} | all-to-all | bytes 8257536 | tf_op jit(solution)/shard_map/all_to_all | solution.py:48
  250.9 1.3 copy.26
  252.3 0.8 pad.4
  253.9 2.9 %copy.29 = bf16[16,8,16,1024]{3,1,2,0:T(8,128)(2,1)S(1)} copy(bf16[16,8,16,1024]{3,2,1,0:T(8,128)(2,1)S(1)} %bitcast.49) | data formatting | bytes 8388608
  256.8 1.2 fusion.25
  258.2 9.2 %psum.7 = f32[1,2,63,63]{3,2,1,0:T(8,128)S(1)} all-reduce(f32[1,2,63,63]{3,2,1,0:T(8,128)S(1)} %maximum_bitcast_fusion), channel_id=1, replica_groups=mesh['freq'=16,'space'=2] {'space'}, use_global_device_ids=true, to_apply=%region_1.2 | all-reduce | flops 7938 | bytes 63504 | tf_op jit(solution)/shard_map/psum | solution.py:55
  268.1 6.7 %copy.28 = bf16[1,16,9,7,1,2,1024]{6,5,1,4,3,2,0:T(2,128)(2,1)S(1)} copy(bf16[1,16,9,7,1,2,1024]{6,5,4,3,2,1,0:T(2,128)(2,1)} %bitcast.40) | data formatting | bytes 8257536 | tf_op jit(solution)/shard_map/all_to_all | solution.py:48
  274.8 1.1 slice_bitcast_fusion
  (27 shorter events, 4.1 us)
Async XLA Ops:
  7.1 7.6 %copy-start.4 = (s32[7]{0:T(128)S(1)}, s32[7]{0:T(128)}, u32[]{:S(2)}) copy-start(s32[7]{0:T(128)} %param.5) | copy-start | bytes 88
  7.1 19.1 %copy-start.5 = (s32[16]{0:T(128)S(1)}, s32[16]{0:T(128)}, u32[]{:S(2)}) copy-start(s32[16]{0:T(128)} %param.6) | copy-start | bytes 196
  7.1 85.2 %all-to-all-start = ((bf16[128,16,1024]{0,2,1:T(8,128)(2,1)}), bf16[128,16,1024]{0,2,1:T(8,128)(2,1)}, u32[]{:S(2)}, u32[]{:S(2)}) async-start(bf16[128,16,1024]{0,2,1:T(8,128)(2,1)} %bitcast.48), calls=%async_computation | async-start | bytes 8388608 | tf_op jit(solution)/shard_map/all_to_all | solution.py:39
  123.9 3.2 %copy-start.1 = (bf16[16,2,9,1,1024]{4,2,1,0,3:T(8,128)(2,1)S(1)}, bf16[16,2,9,1,1024]{4,2,1,0,3:T(8,128)(2,1)}, u32[]{:S(2)}) copy-start(bf16[16,2,9,1,1024]{4,2,1,0,3:T(8,128)(2,1)} %stack_reshape.25) | copy-start | bytes 1769476
  123.9 4.3 %copy-start.2 = (bf16[16,2,9,1,1024]{4,2,1,0,3:T(8,128)(2,1)S(1)}, bf16[16,2,9,1,1024]{4,2,1,0,3:T(8,128)(2,1)}, u32[]{:S(2)}) copy-start(bf16[16,2,9,1,1024]{4,2,1,0,3:T(8,128)(2,1)} %stack_reshape.26) | copy-start | bytes 1769476
  125.0 4.3 %copy-start.3 = (bf16[16,2,9,1,1024]{4,2,1,0,3:T(8,128)(2,1)S(1)}, bf16[16,2,9,1,1024]{4,2,1,0,3:T(8,128)(2,1)}, u32[]{:S(2)}) copy-start(bf16[16,2,9,1,1024]{4,2,1,0,3:T(8,128)(2,1)} %stack_reshape.27) | copy-start | bytes 1769476
  250.9 2.9 %copy-start = (bf16[16,2,9,7,1024]{4,1,3,2,0:T(2,128)(2,1)}, bf16[16,2,9,7,1024]{4,1,3,2,0:T(2,128)(2,1)S(1)}, u32[]{:S(2)}) copy-start(bf16[16,2,9,7,1024]{4,1,3,2,0:T(2,128)(2,1)S(1)} %all_to_all.37) | copy-start | bytes 12386308
where the time goes:
time: 277 us; the launch traced here: 276 us
  blocking collectives  120 us (43%)
  waiting for transfers between devices  59.8 us (22%)
  local copies, waits for them, and re-layouts  54.1 us (20%)
  matrix products  16.7 us (6%)
  between operations  15.5 us (6%)
  starting transfers between devices  7.54 us (3%)
    all_to_all x1, blocking collectives, per_device(): lax.all_to_all(blockspec, 'freq', split_axis=0, concat_axis=4, tiled=True)  111 us
    all_to_all x1, waiting for transfers between devices, per_device(): lax.all_to_all(series, 'freq', split_axis=1, concat_axis=0, tiled=True)  59.8 us
    another operation x9, local copies, waits for them, and re-layouts, per_device(): blockspec = jnp.stack(blocks, axis=3)  19.5 us
    unnamed x22, local copies, waits for them, and re-layouts  18.1 us
    dot_general x7, matrix products, per_device(): jnp.dot(flat_table, block_rows, preferred_element_type=jnp.float32)  15.5 us
    psum x1, blocking collectives, per_device(): gram = lax.psum(gram_part, 'space') / total_cells  9.22 us
    all_to_all x2, local copies, waits for them, and re-layouts, per_device(): lax.all_to_all(blockspec, 'freq', split_axis=0, concat_axis=4, tiled=True)  8.06 us
    all_to_all x1, starting transfers between devices, per_device(): lax.all_to_all(series, 'freq', split_axis=1, concat_axis=0, tiled=True)  7.54 us
  transfers between devices with their start and end apart: 1, of which 1 were waited for; matrix products, arithmetic and copies ran while one was open for 1% of the time, Pallas kernels for 0%

commit v1 on v0

--- a/solution.py
+++ b/solution.py
@@ -45,14 +45,16 @@
         spec_block = jnp.dot(flat_table, block_rows, preferred_element_type=jnp.float32)
         blocks.append(spec_block.astype(jnp.bfloat16).reshape(nfreq, 2, SHIFTS, local_cells))
     blockspec = jnp.stack(blocks, axis=3)
-    received = lax.all_to_all(blockspec, "freq", split_axis=0, concat_axis=4, tiled=True)
-    stacked = received.reshape(2 * order, slab_cells)
+    own_spectra = lax.all_to_all(
+        blockspec[:, :, HALF], "freq", split_axis=0, concat_axis=3, tiled=True
+    )
+    stacked = blockspec.reshape(nfreq, 2 * order, local_cells)
     products = lax.dot_general(
-        stacked, stacked, (((1,), (1,)), ((), ())), preferred_element_type=jnp.float32
+        stacked, stacked, (((2,), (2,)), ((0,), (0,))), preferred_element_type=jnp.float32
     )
-    gram_part = split_quadrants(products, order)[None]
-    own_spectra = received[:, :, HALF]
-    gram = lax.psum(gram_part, "space") / total_cells
+    gram_part = split_quadrants(products, order)
+    gram_own = lax.psum_scatter(gram_part, "freq", scatter_dimension=0, tiled=True)
+    gram = lax.psum(gram_own, "space") / total_cells
     return (own_spectra, gram)
 
 

time: 277 us -> 290 us (1.047)
  blocking collectives: 120 us -> 8.79 us
  waiting for transfers between devices: 59.8 us -> 155 us
  starting transfers between devices: 7.54 us -> 27.2 us
  between operations: 15.5 us -> 29 us
  local copies, waits for them, and re-layouts: 54.1 us -> 45.1 us
  matrix products: 16.7 us -> 19.9 us
    all_to_all x1 -> x0, blocking collectives: 111 us -> none  [per_device(): lax.all_to_all(blockspec, 'freq', split_axis=0, concat_axis=4, tiled=True)]
    unnamed x0 -> x2, waiting for transfers between devices: none -> 95.4 us
    all_to_all x0 -> x1, starting transfers between devices: none -> 19.6 us  [per_device(): lax.all_to_all(blockspec[:, :, HALF], 'freq', split_axis=0, concat_axis=3...]
    all_to_all x2 -> x1, local copies, waits for them, and re-layouts: 8.06 us -> 1.08 us  [per_device(): lax.all_to_all(blockspec[:, :, HALF], 'freq', split_axis=0, concat_axis=3...]
    another operation x9, local copies, waits for them, and re-layouts: 19.5 us -> 15.3 us  [per_device(): blockspec = jnp.stack(blocks, axis=3)]
    slice x0 -> x2, local copies, waits for them, and re-layouts: none -> 3.32 us  [per_device(): blockspec[:, :, HALF]]
    dot_general x1, matrix products: 1.24 us -> 4.42 us  [per_device(): lax.dot_general(stacked, stacked, (((2,), (2,)), ((0,), (0,))), preferred...]
    unnamed x22 -> x21, local copies, waits for them, and re-layouts: 18.1 us -> 14.9 us
  transfers between devices with their start and end apart: 1 -> 3, of which waited for: 1 -> 2; matrix products, arithmetic and copies ran while one was open for 1% -> 3% of each run, Pallas kernels for 0% -> 0%
where the time goes in v1:
time: 290 us; the launch traced here: 288 us
  waiting for transfers between devices  155 us (53%)
  local copies, waits for them, and re-layouts  45.1 us (16%)
  between operations  29 us (10%)
  starting transfers between devices  27.2 us (9%)
  matrix products  19.9 us (7%)
  blocking collectives  8.79 us (3%)
  other arithmetic  3.27 us (1%)
    unnamed x2, waiting for transfers between devices  95.4 us
    all_to_all x1, waiting for transfers between devices, per_device(): lax.all_to_all(series, 'freq', split_axis=1, concat_axis=0, tiled=True)  59.7 us
    all_to_all x1, starting transfers between devices, per_device(): lax.all_to_all(blockspec[:, :, HALF], 'freq', split_axis=0, concat_axis=3...  19.6 us
    dot_general x7, matrix products, per_device(): jnp.dot(flat_table, block_rows, preferred_element_type=jnp.float32)  15.5 us
    another operation x9, local copies, waits for them, and re-layouts, per_device(): blockspec = jnp.stack(blocks, axis=3)  15.3 us
    unnamed x21, local copies, waits for them, and re-layouts  14.9 us
    psum x1, blocking collectives, per_device(): gram = lax.psum(gram_own, 'space') / total_cells  8.79 us
    all_to_all x1, starting transfers between devices, per_device(): lax.all_to_all(series, 'freq', split_axis=1, concat_axis=0, tiled=True)  7.54 us
  transfers between devices with their start and end apart: 3, of which 2 were waited for; matrix products, arithmetic and copies ran while one was open for 3% of the time, Pallas kernels for 0%

profile of v1, /device:TPU:0, one launch (start us, length us, event | category | flops | bytes accessed | tf_op | source)
XLA Modules:
  0.0 288.4 jit_solution(5651149938411296801)
XLA Ops:
  7.2 6.4 %copy.42 = bf16[128,16384]{0,1:T(8,128)(2,1)} copy(bf16[128,16384]{1,0:T(8,128)(2,1)} %param.4) | data formatting | bytes 8388608 | tf_op args[0]
  13.6 7.5 %all-to-all-start = ((bf16[128,16,1024]{0,2,1:T(8,128)(2,1)}), bf16[128,16,1024]{0,2,1:T(8,128)(2,1)}, u32[]{:S(2)}, u32[]{:S(2)}) async-start(bf16[128,16,1024]{0,2,1:T(8,128)(2,1)} %bitcast.40), calls=%async_computation | async-start | bytes 8388608 | tf_op jit(solution)/shard_map/all_to_all | solution.py:39
  32.9 1.4 multiply_convert_fusion
  39.2 59.7 %all-to-all-done = bf16[128,16,1024]{0,2,1:T(8,128)(2,1)} async-done(((bf16[128,16,1024]{0,2,1:T(8,128)(2,1)}), bf16[128,16,1024]{0,2,1:T(8,128)(2,1)}, u32[]{:S(2)}, u32[]{:S(2)}) %all-to-all-start) | async-done | bytes 4194336 | tf_op jit(solution)/shard_map/all_to_all | solution.py:39
  98.8 6.4 %copy.43 = bf16[16,128,1024]{2,1,0:T(8,128)(2,1)} copy(bf16[16,128,1024]{1,2,0:T(8,128)(2,1)} %bitcast.2) | data formatting | bytes 8388608 | tf_op jit(solution)/shard_map/all_to_all | solution.py:39
  105.2 1.7 convolution_convert_fusion.6
  108.2 1.7 convolution_convert_fusion.5
  110.2 1.7 convolution_convert_fusion.4
  112.2 2.6 convolution_convert_fusion.3
  114.8 1.3 stack_reshape.24
  116.1 2.6 convolution_convert_fusion.2
  118.7 2.2 stack_reshape.25
  120.9 2.6 convolution_convert_fusion.1
  123.5 2.2 stack_reshape.26
  125.7 2.6 convolution_convert_fusion
  128.3 2.2 stack_reshape.27
  130.5 1.1 constant_dynamic-update-slice_fusion.5
  131.6 1.1 constant_dynamic-update-slice_fusion.4
  132.6 1.1 constant_dynamic-update-slice_fusion.3
  133.7 1.0 constant_dynamic-update-slice_fusion.2
  134.8 1.1 constant_dynamic-update-slice_fusion.1
  135.8 1.1 constant_dynamic-update-slice_fusion
  136.9 5.6 %copy.47 = bf16[16,2,9,7,1024]{4,0,3,2,1:T(8,128)(2,1)S(1)} copy(bf16[16,2,9,7,1024]{4,2,1,0,3:T(8,128)(2,1)} %constant_dynamic-update-slice_fusion) | data formatting | bytes 8257536 | tf_op jit(solution)/shard_map/stack | solution.py:47
  142.5 3.0 %slice.48 = bf16[16,2,1,7,1024]{4,2,1,0,3:T(2,128)(2,1)S(1)} slice(bf16[16,2,9,7,1024]{4,2,1,0,3:T(8,128)(2,1)} %constant_dynamic-update-slice_fusion), slice={[0:16], [0:2], [4:5], [0:7], [0:1024]} | slice | bytes 917504 | tf_op jit(solution)/shard_map/slice | solution.py:49
  145.6 4.4 %fusion = f32[16,126,126]{2,1,0:T(8,128)S(1)} fusion(bf16[16,126,1024]{2,0,1:T(8,128)(2,1)S(1)} %bitcast.41), kind=kOutput, calls=%fused_computation | convolution fusion | flops 520224768 | bytes 5144832 | tf_op jit(solution)/shard_map/dot_general | solution.py:52
  150.3 1.2 copy.45
  151.5 19.6 %all-to-all-start.1 = ((bf16[16,2,7,1024]{3,1,2,0:T(2,128)(2,1)}), bf16[16,2,7,1024]{3,1,2,0:T(2,128)(2,1)S(1)}, u32[]{:S(2)}, u32[]{:S(2)}) async-start(bf16[16,2,7,1024]{3,1,2,0:T(2,128)(2,1)} %copy.45), calls=%async_computation.1 | async-start | bytes 917504 | tf_op jit(solution)/shard_map/all_to_all | solution.py:48
  171.7 1.8 copy.50
  174.1 95.4 %all-reduce.3.cloned.1.call-done = f32[16,2,63,63]{3,1,2,0:T(2,128)} async-done(((f32[16,2,63,63]{3,1,2,0:T(2,128)}), f32[16,2,63,63]{3,1,2,0:T(2,128)}) %all-reduce.3.cloned.1.call-update) | async-done | bytes 508048
  269.5 1.5 constant_dynamic-slice_fusion
  271.0 8.8 %psum.7 = f32[1,2,63,63]{3,1,2,0:T(2,128)S(1)} all-reduce(f32[1,2,63,63]{3,1,2,0:T(2,128)S(1)} %constant_dynamic-slice_fusion), channel_id=1, replica_groups=mesh['freq'=16,'space'=2] {'space'}, use_global_device_ids=true, to_apply=%region_2.3 | all-reduce | flops 7938 | bytes 63504 | tf_op jit(solution)/shard_map/psum | solution.py:57
  280.5 1.1 copy.51
  (32 shorter events, 5.6 us)
Async XLA Ops:
  13.6 7.6 %copy-start.3 = (s32[7]{0:T(128)S(1)}, s32[7]{0:T(128)}, u32[]{:S(2)}) copy-start(s32[7]{0:T(128)} %param.5) | copy-start | bytes 88
  13.6 19.2 %copy-start.4 = (s32[16]{0:T(128)S(1)}, s32[16]{0:T(128)}, u32[]{:S(2)}) copy-start(s32[16]{0:T(128)} %param.6) | copy-start | bytes 196
  13.6 85.2 %all-to-all-start = ((bf16[128,16,1024]{0,2,1:T(8,128)(2,1)}), bf16[128,16,1024]{0,2,1:T(8,128)(2,1)}, u32[]{:S(2)}, u32[]{:S(2)}) async-start(bf16[128,16,1024]{0,2,1:T(8,128)(2,1)} %bitcast.40), calls=%async_computation | async-start | bytes 8388608 | tf_op jit(solution)/shard_map/all_to_all | solution.py:39
  130.5 3.2 %copy-start = (bf16[16,2,9,1,1024]{4,2,1,0,3:T(8,128)(2,1)S(1)}, bf16[16,2,9,1,1024]{4,2,1,0,3:T(8,128)(2,1)}, u32[]{:S(2)}) copy-start(bf16[16,2,9,1,1024]{4,2,1,0,3:T(8,128)(2,1)} %stack_reshape.25) | copy-start | bytes 1769476
  130.5 4.3 %copy-start.1 = (bf16[16,2,9,1,1024]{4,2,1,0,3:T(8,128)(2,1)S(1)}, bf16[16,2,9,1,1024]{4,2,1,0,3:T(8,128)(2,1)}, u32[]{:S(2)}) copy-start(bf16[16,2,9,1,1024]{4,2,1,0,3:T(8,128)(2,1)} %stack_reshape.26) | copy-start | bytes 1769476
  131.6 4.3 %copy-start.2 = (bf16[16,2,9,1,1024]{4,2,1,0,3:T(8,128)(2,1)S(1)}, bf16[16,2,9,1,1024]{4,2,1,0,3:T(8,128)(2,1)}, u32[]{:S(2)}) copy-start(bf16[16,2,9,1,1024]{4,2,1,0,3:T(8,128)(2,1)} %stack_reshape.27) | copy-start | bytes 1769476
  151.5 129.0 %all-to-all-start.1 = ((bf16[16,2,7,1024]{3,1,2,0:T(2,128)(2,1)}), bf16[16,2,7,1024]{3,1,2,0:T(2,128)(2,1)S(1)}, u32[]{:S(2)}, u32[]{:S(2)}) async-start(bf16[16,2,7,1024]{3,1,2,0:T(2,128)(2,1)} %copy.45), calls=%async_computation.1 | async-start | bytes 917504 | tf_op jit(solution)/shard_map/all_to_all | solution.py:48
  171.2 2.4 copy-start.5
  171.2 98.4 %all-reduce.3.cloned.1.call-start = ((), (), s32[]{:S(2)}) async-start(), calls=%async_computation.2 | async-start | bytes 2064384
Sparse Core Ops, SparseCore 0:
  175.5 94.0 all-reduce.2

commit v2 on v0

v2 whole, which is shorter than its diff:
```python
import functools
import math

import jax
import jax.numpy as jnp
from jax import lax
from jax.experimental import pallas as pl
from jax.experimental.pallas import tpu as pltpu
from jax.sharding import PartitionSpec as P

NFFT = 512
NBLK = 7
HALF = 4
SHIFTS = 9
ORDER = SHIFTS * NBLK
QUAD = 64
GRAM_ROWS = 2 * QUAD
OWN_ROWS = 16
FREQ_ROWS = GRAM_ROWS + OWN_ROWS
GROUP = 4
MESH = pl.DeviceIdType.MESH


def half_turn_sine(steps):
    x = steps.astype(jnp.float32) * (math.pi / 256.0)
    x2 = x * x
    p = -1.0 / math.factorial(11)
    for order in (9, 7, 5, 3, 1):
        p = p * x2 + (-1.0) ** ((order - 1) // 2) / math.factorial(order)
    return p * x


def negative_cosine(step):
    folded = 128 - jnp.abs((step & (NFFT - 1)) - NFFT // 2)
    return half_turn_sine(folded)


def row_fields(starts):
    row = lax.broadcasted_iota(jnp.int32, (FREQ_ROWS, 128), 0)
    own = row >= GRAM_ROWS
    half = jnp.where(own, GRAM_ROWS + OWN_ROWS // 2, QUAD)
    part = jnp.where(row >= half, 1, 0)
    inner = jnp.where(own, row - GRAM_ROWS - OWN_ROWS // 2 * part, row - QUAD * part)
    shift = jnp.zeros_like(row)
    for bound in range(1, SHIFTS + 1):
        shift += jnp.where(inner >= NBLK * bound, 1, 0)
    block = jnp.where(own, inner, inner - NBLK * shift)
    used = inner < jnp.where(own, NBLK, ORDER)
    shift = jnp.where(own, HALF, shift)
    first = jnp.zeros_like(row)
    for index in range(NBLK):
        first = jnp.where(block == index, starts[index], first)
    return shift, part, first, used


def kernel(
    n,
    ns,
    nfreq,
    nchunk,
    total_cells,
    starts_ref,
    freqs_ref,
    alpha_ref,
    series_ref,
    spec_ref,
    gram_ref,
    table,
    weight,
    elapsed,
    spread,
    stage,
    accum,
    pack_out,
    pack_in,
    space_parts,
    raw_send,
    raw_recv,
    spec_send,
    spec_recv,
    gram_send,
    gram_recv,
    space_send,
    space_recv,
    local_sem,
    *slabs,
):
    me = lax.axis_index("freq")
    my_space = lax.axis_index("space")
    rows, slab_cells = series_ref.shape
    nt = rows * n
    own_cells = slab_cells // n
    width = own_cells // nchunk

    def at_freq(peer):
        return {"freq": peer, "space": my_space}

    def at_space(peer):
        return {"freq": me, "space": peer}

    barrier = pltpu.get_barrier_semaphore()

    @pl.loop(1, n)
    def _(k):
        pl.semaphore_signal(
            barrier, inc=1, device_id=at_freq(lax.rem(me + k, n)), device_id_type=MESH
        )

    @pl.loop(1, ns)
    def _(k):
        pl.semaphore_signal(
            barrier, inc=1, device_id=at_space(lax.rem(my_space + k, ns)), device_id_type=MESH
        )

    pl.semaphore_wait(barrier, n + ns - 2)

    def raw_copy(c, peer, slot):
        cells = pl.ds(pl.multiple_of(peer * own_cells + c * width, 128), width)
        mine = pl.ds(pl.multiple_of(me * rows, rows), rows)
        return pltpu.make_async_remote_copy(
            src_ref=series_ref.at[:, cells],
            dst_ref=slabs[c].at[mine, :],
            send_sem=raw_send.at[c, peer],
            recv_sem=raw_recv.at[c, slot],
            device_id=at_freq(peer),
            device_id_type=MESH,
        )

    def own_copy(c):
        cells = pl.ds(pl.multiple_of(me * own_cells + c * width, 128), width)
        mine = pl.ds(pl.multiple_of(me * rows, rows), rows)
        return pltpu.make_async_copy(
            series_ref.at[:, cells], slabs[c].at[mine, :], local_sem.at[0, c]
        )

    def spec_copy(c, peer, slot):
        cells = pl.ds(pl.multiple_of(me * own_cells + c * width, 128), width)
        return pltpu.make_async_remote_copy(
            src_ref=stage.at[c, peer],
            dst_ref=spec_ref.at[:, cells],
            send_sem=spec_send.at[c, peer],
            recv_sem=spec_recv.at[c, slot],
            device_id=at_freq(peer),
            device_id_type=MESH,
        )

    def own_spec_copy(c):
        cells = pl.ds(pl.multiple_of(me * own_cells + c * width, 128), width)
        return pltpu.make_async_copy(
            stage.at[c, me], spec_ref.at[:, cells], local_sem.at[1, c]
        )

    def gram_copy(peer, slot):
        return pltpu.make_async_remote_copy(
            src_ref=pack_out.at[peer],
            dst_ref=pack_in.at[me],
            send_sem=gram_send.at[peer],
            recv_sem=gram_recv.at[slot],
            device_id=at_freq(peer),
            device_id_type=MESH,
        )

    def space_copy(peer, slot):
        return pltpu.make_async_remote_copy(
            src_ref=space_parts.at[my_space],
            dst_ref=space_parts.at[my_space],
            send_sem=space_send.at[peer],
            recv_sem=space_recv.at[slot],
            device_id=at_space(peer),
            device_id_type=MESH,
        )

    for c in range(nchunk):

        @pl.loop(1, n)
        def _(k):
            raw_copy(c, lax.rem(me + k, n), me).start()

        own_copy(c).start()

    shift, part, first, used = row_fields([starts_ref[b] for b in range(NBLK)])
    quarter = part * (NFFT // 4)
    scale = 0.5 / math.sqrt(0.375 * NFFT)
    lane = lax.broadcasted_iota(jnp.int32, (FREQ_ROWS, 128), 1)

    @pl.loop(0, nt // 128)
    def _(i):
        cols = pl.ds(pl.multiple_of(i * 128, 128), 128)
        t = lane + i * 128 - first
        inside = (t >= 0) & (t < NFFT) & used
        window = scale + scale * negative_cosine(t)
        elapsed[:, cols] = t
        weight[:, cols] = jnp.where(inside, -window, 0.0)

    @pl.loop(0, nfreq)
    def _(j):
        bins = freqs_ref[j] + (shift - HALF) * alpha_ref[0]
        base = pl.multiple_of(j * FREQ_ROWS, 16)

        @pl.loop(0, nt // 128)
        def _(i):
            cols = pl.ds(pl.multiple_of(i * 128, 128), 128)
            step = bins * elapsed[:, cols] + quarter
            value = negative_cosine(step) * weight[:, cols]
            table[pl.ds(base, FREQ_ROWS), cols] = value.astype(jnp.bfloat16)

    for c in range(nchunk):
        own_copy(c).wait()

        @pl.loop(1, n)
        def _(k):
            peer = lax.rem(me + k, n)
            raw_copy(c, peer, peer).wait_recv()

        @pl.loop(0, nfreq // GROUP)
        def _(g):
            base = pl.multiple_of(g * (GROUP * FREQ_ROWS), 16)
            result = jnp.dot(
                table[pl.ds(base, GROUP * FREQ_ROWS), :],
                slabs[c][...],
                preferred_element_type=jnp.float32,
            ).astype(jnp.bfloat16)
            for i in range(GROUP):
                j = g * GROUP + i
                spread[j] = result[i * FREQ_ROWS : i * FREQ_ROWS + GRAM_ROWS]
                stage[c, j] = result[i * FREQ_ROWS + GRAM_ROWS : (i + 1) * FREQ_ROWS]

        @pl.loop(1, n)
        def _(k):
            peer = lax.rem(me + k, n)
            spec_copy(c, peer, me).start()

        own_spec_copy(c).start()

        @pl.loop(0, nfreq)
        def _(j):
            lines = spread[j]
            product = lax.dot_general(
                lines, lines, (((1,), (1,)), ((), ())), preferred_element_type=jnp.float32
            )
            if c == 0:
                accum[j] = product
            else:
                accum[j] += product

    prow = lax.broadcasted_iota(jnp.int32, (QUAD, 128), 0)
    pcol = lax.broadcasted_iota(jnp.int32, (QUAD, 128), 1)
    left = lax.broadcasted_iota(jnp.int32, (QUAD // 2, 128), 1) < QUAD

    @pl.loop(0, nfreq)
    def _(j):
        whole = accum[j]
        turned = pltpu.roll(whole, QUAD, 1)
        real = whole[:QUAD] + turned[QUAD:]
        imag = turned[:QUAD] - whole[QUAD:]
        mixed = jnp.where(prow <= pcol, real, imag)
        low = pltpu.roll(mixed[QUAD // 2 :], QUAD, 1)
        pack_out[j] = jnp.where(left, mixed[: QUAD // 2], low).astype(jnp.bfloat16)

    pack_in[me] = pack_out[me]

    @pl.loop(1, n)
    def _(k):
        gram_copy(lax.rem(me + k, n), me).start()

    @pl.loop(1, n)
    def _(k):
        peer = lax.rem(me + k, n)
        gram_copy(peer, peer).wait_recv()

    total = pack_in[0].astype(jnp.float32)
    for p in range(1, n):
        total += pack_in[p].astype(jnp.float32)
    space_parts[my_space] = total

    @pl.loop(1, ns)
    def _(k):
        space_copy(lax.rem(my_space + k, ns), my_space).start()

    @pl.loop(1, ns)
    def _(k):
        peer = lax.rem(my_space + k, ns)
        pltpu.make_async_remote_copy(
            src_ref=space_parts.at[my_space],
            dst_ref=space_parts.at[peer],
            send_sem=space_send.at[peer],
            recv_sem=space_recv.at[peer],
            device_id=at_space(peer),
            device_id_type=MESH,
        ).wait_recv()

    total = space_parts[0]
    for p in range(1, ns):
        total += space_parts[p]
    total = total * (1.0 / total_cells)
    mixed = jnp.concatenate(
        [total, pltpu.roll(total, QUAD, 1), jnp.zeros((QUAD, 128), jnp.float32)], axis=0
    )
    flipped = mixed.T[:QUAD]
    mixed = mixed[:QUAD]
    real = jnp.where(prow <= pcol, mixed, flipped)
    imag = jnp.where(prow > pcol, mixed, jnp.where(prow == pcol, 0.0, -flipped))
    gram_ref[0, 0] = real[:ORDER, :ORDER]
    gram_ref[0, 1] = imag[:ORDER, :ORDER]

    for c in range(nchunk):
        own_spec_copy(c).wait()

        @pl.loop(1, n)
        def _(k):
            peer = lax.rem(me + k, n)
            spec_copy(c, peer, peer).wait_recv()

    for c in range(nchunk):

        @pl.loop(1, n)
        def _(k):
            peer = lax.rem(me + k, n)
            raw_copy(c, peer, me).wait_send()
            spec_copy(c, peer, me).wait_send()

    @pl.loop(1, n)
    def _(k):
        peer = lax.rem(me + k, n)
        gram_copy(peer, me).wait_send()

    @pl.loop(1, ns)
    def _(k):
        space_copy(lax.rem(my_space + k, ns), my_space).wait_send()


def solution(mesh):
    n = mesh.shape["freq"]
    ns = mesh.shape["space"]

    def per_device(series, starts, freqs, alpha):
        rows, slab_cells = series.shape
        nfreq = freqs.shape[0]
        nt = rows * n
        own_cells = slab_cells // n
        nchunk = max(2, own_cells // 256)
        width = own_cells // nchunk
        smem = pl.BlockSpec(memory_space=pltpu.SMEM)
        table_rows = nfreq * FREQ_ROWS
        cost = pl.CostEstimate(
            flops=2 * table_rows * nt * own_cells,
            bytes_accessed=2 * rows * slab_cells * 2,
            transcendentals=0,
        )
        dma = pltpu.SemaphoreType.DMA
        spec, gram = pl.pallas_call(
            functools.partial(kernel, n, ns, nfreq, nchunk, slab_cells * ns),
            out_shape=(
                jax.ShapeDtypeStruct((OWN_ROWS, slab_cells), jnp.bfloat16),
                jax.ShapeDtypeStruct((1, 2, ORDER, ORDER), jnp.float32),
            ),
            in_specs=[smem, smem, smem, pl.BlockSpec(memory_space=pl.ANY)],
            out_specs=(
                pl.BlockSpec(memory_space=pl.ANY),
                pl.BlockSpec(memory_space=pltpu.VMEM),
            ),
            scratch_shapes=[
                pltpu.VMEM((table_rows, nt), jnp.bfloat16),
                pltpu.VMEM((FREQ_ROWS, nt), jnp.float32),
                pltpu.VMEM((FREQ_ROWS, nt), jnp.int32),
                pltpu.VMEM((nfreq, GRAM_ROWS, width), jnp.bfloat16),
                pltpu.VMEM((nchunk, nfreq, OWN_ROWS, width), jnp.bfloat16),
                pltpu.VMEM((nfreq, GRAM_ROWS, GRAM_ROWS), jnp.float32),
                pltpu.VMEM((nfreq, QUAD // 2, 128), jnp.bfloat16),
                pltpu.VMEM((n, QUAD // 2, 128), jnp.bfloat16),
                pltpu.VMEM((ns, QUAD // 2, 128), jnp.float32),
                dma((nchunk, n)),
                dma((nchunk, n)),
                dma((nchunk, n)),
                dma((nchunk, n)),
                dma((n,)),
                dma((n,)),
                dma((ns,)),
                dma((ns,)),
                dma((2, nchunk)),
            ]
            + [pltpu.VMEM((nt, width), jnp.bfloat16)] * nchunk,
            compiler_params=pltpu.CompilerParams(
                collective_id=0, has_side_effects=True, vmem_limit_bytes=60 * 1024 * 1024
            ),
            cost_estimate=cost,
        )(starts, freqs, alpha, series)
        own = spec.reshape(2, OWN_ROWS // 2, slab_cells)[:, :NBLK]
        return own[None], gram

    placed = (P("freq", "space"), P(), P(), P())
    return jax.shard_map(
        per_device,
        mesh=mesh,
        in_specs=placed,
        out_specs=(P("freq", None, None, "space"), P("freq", None, None, None)),
        check_vma=False,
    )
```

time: 277 us -> 132 us (0.48)
  Pallas kernels: 0 us -> 127 us
  blocking collectives: 120 us -> 0 us
  waiting for transfers between devices: 59.8 us -> 0 us
  local copies, waits for them, and re-layouts: 54.1 us -> 3.83 us
  matrix products: 16.7 us -> 0 us
  between operations: 15.5 us -> 1.29 us
  starting transfers between devices: 7.54 us -> 0 us
    pallas_call x0 -> x1, Pallas kernels: none -> 127 us  [per_device(): pl.pallas_call(functools.partial(kernel, n, ns, nfreq, nchunk, slab_cells...]
    all_to_all x1 -> x0, blocking collectives: 111 us -> none  [per_device(): lax.all_to_all(blockspec, 'freq', split_axis=0, concat_axis=4, tiled=True)]
    all_to_all x1 -> x0, waiting for transfers between devices: 59.8 us -> none  [per_device(): lax.all_to_all(series, 'freq', split_axis=1, concat_axis=0, tiled=True)]
    another operation x10 -> x0, local copies, waits for them, and re-layouts: 19.7 us -> none  [the longest x9 19.5 us: per_device(): blockspec = jnp.stack(blocks, axis=3)]
    dot_general x8 -> x0, matrix products: 16.7 us -> none  [the longest x7 15.5 us: per_device(): jnp.dot(flat_table, block_rows, preferred_element_type=jnp.float32)]
    all_to_all x3 -> x0, local copies, waits for them, and re-layouts: 14.5 us -> none  [the longest x2 8.06 us: per_device(): lax.all_to_all(blockspec, 'freq', split_axis=0, concat_axis=4, tiled=True)]
    unnamed x22 -> x2, local copies, waits for them, and re-layouts: 18.1 us -> 3.83 us
    psum x1 -> x0, blocking collectives: 9.22 us -> none  [per_device(): gram = lax.psum(gram_part, 'space') / total_cells]
  transfers between devices with their start and end apart: 1 -> 0, of which waited for: 1 -> 0; matrix products, arithmetic and copies ran while one was open for 1% -> 0% of each run, Pallas kernels for 0% -> 0%
where the time goes in v2:
time: 132 us
  Pallas kernels  127 us (96%)
  local copies, waits for them, and re-layouts  3.83 us (3%)
    pallas_call x1, Pallas kernels, per_device(): pl.pallas_call(functools.partial(kernel, n, ns, nfreq, nchunk, slab_cells...  127 us
    unnamed x2, local copies, waits for them, and re-layouts  3.83 us

profile of v2, /device:TPU:0, one launch (start us, length us, event | category | flops | bytes accessed | tf_op | source)
XLA Modules:
  0.0 131.9 jit_solution(9595527683956772982)
XLA Ops:
  1.3 126.8 %shard_map.59 = (bf16[16,16384]{1,0:T(8,128)(2,1)}, f32[1,2,63,63]{3,2,1,0:T(8,128)}) custom-call(s32[7]{0:T(128)} %starts_ref.1, s32[16]{0:T(128)} %freqs_ref.1, s32[1]{0:T(128)S(6)} %copy.11.alpha_ref, bf16[128,16384]{1,0:T(8,128)(2,1)} %series_ref.1), custom_call_target="tpu_custom_call" | custom-call | flops 9663676416 | bytes 8388608 | tf_op jit(solution)/shard_map/pallas_call | solution.py:351
  128.1 2.3 %copy.10 = bf16[2,7,16384]{2,0,1:T(2,128)(2,1)} copy(bf16[2,7,16384]{2,1,0:T(8,128)(2,1)} %bitcast.5) | data formatting | bytes 917504
  130.4 1.5 %copy.7 = f32[1,2,63,63]{3,1,2,0:T(2,128)} copy(f32[1,2,63,63]{3,2,1,0:T(8,128)} %get-tuple-element.7) | data formatting | bytes 63504

commit v3 on v2

--- a/solution.py
+++ b/solution.py
@@ -68,7 +68,6 @@
     table,
     weight,
     elapsed,
-    spread,
     stage,
     accum,
     pack_out,
@@ -172,11 +171,25 @@
 
     for c in range(nchunk):
 
-        @pl.loop(1, n)
+        @pl.loop(0, n - 1)
         def _(k):
-            raw_copy(c, lax.rem(me + k, n), me).start()
+            away = 1 + lax.rem(k + n // 2 - 1, n - 1)
+            raw_copy(c, lax.rem(me + away, n), me).start()
 
         own_copy(c).start()
+
+    groups = nfreq // GROUP
+    prow = lax.broadcasted_iota(jnp.int32, (QUAD, 128), 0)
+    pcol = lax.broadcasted_iota(jnp.int32, (QUAD, 128), 1)
+    left = lax.broadcasted_iota(jnp.int32, (QUAD // 2, 128), 1) < QUAD
+
+    def packed(whole):
+        turned = pltpu.roll(whole, QUAD, 1)
+        real = whole[:QUAD] + turned[QUAD:]
+        imag = turned[:QUAD] - whole[QUAD:]
+        mixed = jnp.where(prow <= pcol, real, imag)
+        low = pltpu.roll(mixed[QUAD // 2 :], QUAD, 1)
+        return jnp.where(left, mixed[: QUAD // 2], low).astype(jnp.bfloat16)
 
     shift, part, first, used = row_fields([starts_ref[b] for b in range(NBLK)])
     quarter = part * (NFFT // 4)
@@ -212,8 +225,11 @@
             peer = lax.rem(me + k, n)
             raw_copy(c, peer, peer).wait_recv()
 
-        @pl.loop(0, nfreq // GROUP)
-        def _(g):
+        last = c == nchunk - 1
+
+        @pl.loop(0, groups)
+        def _(step):
+            g = lax.rem(step + lax.div(me, GROUP) + groups // 2, groups)
             base = pl.multiple_of(g * (GROUP * FREQ_ROWS), 16)
             result = jnp.dot(
                 table[pl.ds(base, GROUP * FREQ_ROWS), :],
@@ -222,46 +238,29 @@
             ).astype(jnp.bfloat16)
             for i in range(GROUP):
                 j = g * GROUP + i
-                spread[j] = result[i * FREQ_ROWS : i * FREQ_ROWS + GRAM_ROWS]
+                lines = result[i * FREQ_ROWS : i * FREQ_ROWS + GRAM_ROWS]
                 stage[c, j] = result[i * FREQ_ROWS + GRAM_ROWS : (i + 1) * FREQ_ROWS]
-
-        @pl.loop(1, n)
-        def _(k):
-            peer = lax.rem(me + k, n)
-            spec_copy(c, peer, me).start()
+                product = lax.dot_general(
+                    lines, lines, (((1,), (1,)), ((), ())), preferred_element_type=jnp.float32
+                )
+                if c > 0:
+                    product += accum[j]
+                if last:
+                    pack_out[j] = packed(product)
+                else:
+                    accum[j] = product
+            for i in range(GROUP):
+                j = g * GROUP + i
+
+                @pl.when(j != me)
+                def _():
+                    if last:
+                        gram_copy(j, me).start()
+                    spec_copy(c, j, me).start()
 
         own_spec_copy(c).start()
 
-        @pl.loop(0, nfreq)
-        def _(j):
-            lines = spread[j]
-            product = lax.dot_general(
-                lines, lines, (((1,), (1,)), ((), ())), preferred_element_type=jnp.float32
-            )
-            if c == 0:
-                accum[j] = product
-            else:
-                accum[j] += product
-
-    prow = lax.broadcasted_iota(jnp.int32, (QUAD, 128), 0)
-    pcol = lax.broadcasted_iota(jnp.int32, (QUAD, 128), 1)
-    left = lax.broadcasted_iota(jnp.int32, (QUAD // 2, 128), 1) < QUAD
-
-    @pl.loop(0, nfreq)
-    def _(j):
-        whole = accum[j]
-        turned = pltpu.roll(whole, QUAD, 1)
-        real = whole[:QUAD] + turned[QUAD:]
-        imag = turned[:QUAD] - whole[QUAD:]
-        mixed = jnp.where(prow <= pcol, real, imag)
-        low = pltpu.roll(mixed[QUAD // 2 :], QUAD, 1)
-        pack_out[j] = jnp.where(left, mixed[: QUAD // 2], low).astype(jnp.bfloat16)
-
     pack_in[me] = pack_out[me]
-
-    @pl.loop(1, n)
-    def _(k):
-        gram_copy(lax.rem(me + k, n), me).start()
 
     @pl.loop(1, n)
     def _(k):
@@ -363,7 +362,6 @@
                 pltpu.VMEM((table_rows, nt), jnp.bfloat16),
                 pltpu.VMEM((FREQ_ROWS, nt), jnp.float32),
                 pltpu.VMEM((FREQ_ROWS, nt), jnp.int32),
-                pltpu.VMEM((nfreq, GRAM_ROWS, width), jnp.bfloat16),
                 pltpu.VMEM((nchunk, nfreq, OWN_ROWS, width), jnp.bfloat16),
                 pltpu.VMEM((nfreq, GRAM_ROWS, GRAM_ROWS), jnp.float32),
                 pltpu.VMEM((nfreq, QUAD // 2, 128), jnp.bfloat16),

time: 132 us -> 126 us (0.955)
  Pallas kernels: 127 us -> 121 us
    pallas_call x1, Pallas kernels: 127 us -> 121 us  [per_device(): pl.pallas_call(functools.partial(kernel, n, ns, nfreq, nchunk, slab_cells...]
where the time goes in v3:
time: 126 us
  Pallas kernels  121 us (96%)
  local copies, waits for them, and re-layouts  3.83 us (3%)
  between operations  1.29 us (1%)
    pallas_call x1, Pallas kernels, per_device(): pl.pallas_call(functools.partial(kernel, n, ns, nfreq, nchunk, slab_cells...  121 us
    unnamed x2, local copies, waits for them, and re-layouts  3.83 us

profile of v3, /device:TPU:0, one launch (start us, length us, event | category | flops | bytes accessed | tf_op | source)
XLA Modules:
  0.0 125.7 jit_solution(11871762748859324285)
XLA Ops:
  1.3 120.6 %shard_map.59 = (bf16[16,16384]{1,0:T(8,128)(2,1)}, f32[1,2,63,63]{3,2,1,0:T(8,128)}) custom-call(s32[7]{0:T(128)} %starts_ref.1, s32[16]{0:T(128)} %freqs_ref.1, s32[1]{0:T(128)S(6)} %copy.11.alpha_ref, bf16[128,16384]{1,0:T(8,128)(2,1)} %series_ref.1), custom_call_target="tpu_custom_call" | custom-call | flops 9663676416 | bytes 8388608 | tf_op jit(solution)/shard_map/pallas_call | solution.py:350
  121.9 2.3 %copy.10 = bf16[2,7,16384]{2,0,1:T(2,128)(2,1)} copy(bf16[2,7,16384]{2,1,0:T(8,128)(2,1)} %bitcast.5) | data formatting | bytes 917504
  124.2 1.5 %copy.7 = f32[1,2,63,63]{3,1,2,0:T(2,128)} copy(f32[1,2,63,63]{3,2,1,0:T(8,128)} %get-tuple-element.7) | data formatting | bytes 63504

commit v4 on v3

--- a/solution.py
+++ b/solution.py
@@ -18,6 +18,7 @@
 OWN_ROWS = 16
 FREQ_ROWS = GRAM_ROWS + OWN_ROWS
 GROUP = 4
+AHEAD = 2
 MESH = pl.DeviceIdType.MESH
 
 
@@ -169,14 +170,16 @@
             device_id_type=MESH,
         )
 
-    for c in range(nchunk):
-
+    def start_chunk(c):
         @pl.loop(0, n - 1)
         def _(k):
             away = 1 + lax.rem(k + n // 2 - 1, n - 1)
             raw_copy(c, lax.rem(me + away, n), me).start()
 
         own_copy(c).start()
+
+    for c in range(AHEAD):
+        start_chunk(c)
 
     groups = nfreq // GROUP
     prow = lax.broadcasted_iota(jnp.int32, (QUAD, 128), 0)
@@ -224,6 +227,13 @@
         def _(k):
             peer = lax.rem(me + k, n)
             raw_copy(c, peer, peer).wait_recv()
+
+        @pl.loop(1, n)
+        def _(k):
+            raw_copy(c, lax.rem(me + k, n), me).wait_send()
+
+        if c + AHEAD < nchunk:
+            start_chunk(c + AHEAD)
 
         last = c == nchunk - 1
 
@@ -315,7 +325,6 @@
         @pl.loop(1, n)
         def _(k):
             peer = lax.rem(me + k, n)
-            raw_copy(c, peer, me).wait_send()
             spec_copy(c, peer, me).wait_send()
 
     @pl.loop(1, n)

time: 126 us -> 127 us (level)
    pallas_call x1, Pallas kernels: 121 us -> 122 us  [per_device(): pl.pallas_call(functools.partial(kernel, n, ns, nfreq, nchunk, slab_cells...]
where the time goes in v4:
time: 127 us
  Pallas kernels  122 us (96%)
  local copies, waits for them, and re-layouts  3.83 us (3%)
  between operations  1.29 us (1%)
    pallas_call x1, Pallas kernels, per_device(): pl.pallas_call(functools.partial(kernel, n, ns, nfreq, nchunk, slab_cells...  122 us
    unnamed x2, local copies, waits for them, and re-layouts  3.83 us

profile of v4, /device:TPU:0, one launch (start us, length us, event | category | flops | bytes accessed | tf_op | source)
XLA Modules:
  0.0 127.2 jit_solution(12007138515767608562)
XLA Ops:
  1.3 122.1 %shard_map.59 = (bf16[16,16384]{1,0:T(8,128)(2,1)}, f32[1,2,63,63]{3,2,1,0:T(8,128)}) custom-call(s32[7]{0:T(128)} %starts_ref.1, s32[16]{0:T(128)} %freqs_ref.1, s32[1]{0:T(128)S(6)} %copy.11.alpha_ref, bf16[128,16384]{1,0:T(8,128)(2,1)} %series_ref.1), custom_call_target="tpu_custom_call" | custom-call | flops 9663676416 | bytes 8388608 | tf_op jit(solution)/shard_map/pallas_call | solution.py:359
  123.4 2.3 %copy.10 = bf16[2,7,16384]{2,0,1:T(2,128)(2,1)} copy(bf16[2,7,16384]{2,1,0:T(8,128)(2,1)} %bitcast.5) | data formatting | bytes 917504
  125.7 1.5 %copy.7 = f32[1,2,63,63]{3,1,2,0:T(2,128)} copy(f32[1,2,63,63]{3,2,1,0:T(8,128)} %get-tuple-element.7) | data formatting | bytes 63504

commit v5 on v3

--- a/solution.py
+++ b/solution.py
@@ -38,9 +38,8 @@
 def row_fields(starts):
     row = lax.broadcasted_iota(jnp.int32, (FREQ_ROWS, 128), 0)
     own = row >= GRAM_ROWS
-    half = jnp.where(own, GRAM_ROWS + OWN_ROWS // 2, QUAD)
-    part = jnp.where(row >= half, 1, 0)
-    inner = jnp.where(own, row - GRAM_ROWS - OWN_ROWS // 2 * part, row - QUAD * part)
+    part = jnp.where(own, row & 1, jnp.where(row >= QUAD, 1, 0))
+    inner = jnp.where(own, (row - GRAM_ROWS) >> 1, row - QUAD * part)
     shift = jnp.zeros_like(row)
     for bound in range(1, SHIFTS + 1):
         shift += jnp.where(inner >= NBLK * bound, 1, 0)
@@ -69,6 +68,7 @@
     weight,
     elapsed,
     stage,
+    outgoing,
     accum,
     pack_out,
     pack_in,
@@ -82,6 +82,7 @@
     space_send,
     space_recv,
     local_sem,
+    stage_sem,
     *slabs,
 ):
     me = lax.axis_index("freq")
@@ -97,6 +98,15 @@
     def at_space(peer):
         return {"freq": me, "space": peer}
 
+    def stage_copy(c, peer):
+        cells = pl.ds(pl.multiple_of(peer * own_cells + c * width, 128), width)
+        return pltpu.make_async_copy(
+            series_ref.at[:, cells], outgoing.at[c, peer], stage_sem.at[c, peer]
+        )
+
+    def peer_at(k):
+        return lax.rem(me + 1 + lax.rem(k + n // 2 - 1, n - 1), n)
+
     barrier = pltpu.get_barrier_semaphore()
 
     @pl.loop(1, n)
@@ -111,13 +121,18 @@
             barrier, inc=1, device_id=at_space(lax.rem(my_space + k, ns)), device_id_type=MESH
         )
 
+    for c in range(nchunk):
+
+        @pl.loop(0, n - 1)
+        def _(k):
+            stage_copy(c, peer_at(k)).start()
+
     pl.semaphore_wait(barrier, n + ns - 2)
 
     def raw_copy(c, peer, slot):
-        cells = pl.ds(pl.multiple_of(peer * own_cells + c * width, 128), width)
         mine = pl.ds(pl.multiple_of(me * rows, rows), rows)
         return pltpu.make_async_remote_copy(
-            src_ref=series_ref.at[:, cells],
+            src_ref=outgoing.at[c, peer],
             dst_ref=slabs[c].at[mine, :],
             send_sem=raw_send.at[c, peer],
             recv_sem=raw_recv.at[c, slot],
@@ -136,7 +151,7 @@
         cells = pl.ds(pl.multiple_of(me * own_cells + c * width, 128), width)
         return pltpu.make_async_remote_copy(
             src_ref=stage.at[c, peer],
-            dst_ref=spec_ref.at[:, cells],
+            dst_ref=spec_ref.at[:, :, cells],
             send_sem=spec_send.at[c, peer],
             recv_sem=spec_recv.at[c, slot],
             device_id=at_freq(peer),
@@ -146,7 +161,7 @@
     def own_spec_copy(c):
         cells = pl.ds(pl.multiple_of(me * own_cells + c * width, 128), width)
         return pltpu.make_async_copy(
-            stage.at[c, me], spec_ref.at[:, cells], local_sem.at[1, c]
+            stage.at[c, me], spec_ref.at[:, :, cells], local_sem.at[1, c]
         )
 
     def gram_copy(peer, slot):
@@ -173,8 +188,9 @@
 
         @pl.loop(0, n - 1)
         def _(k):
-            away = 1 + lax.rem(k + n // 2 - 1, n - 1)
-            raw_copy(c, lax.rem(me + away, n), me).start()
+            peer = peer_at(k)
+            stage_copy(c, peer).wait()
+            raw_copy(c, peer, me).start()
 
         own_copy(c).start()
 
@@ -239,7 +255,8 @@
             for i in range(GROUP):
                 j = g * GROUP + i
                 lines = result[i * FREQ_ROWS : i * FREQ_ROWS + GRAM_ROWS]
-                stage[c, j] = result[i * FREQ_ROWS + GRAM_ROWS : (i + 1) * FREQ_ROWS]
+                first = i * FREQ_ROWS + GRAM_ROWS
+                stage[c, j] = result[first : first + 2 * NBLK].reshape(NBLK, 2, width)
                 product = lax.dot_general(
                     lines, lines, (((1,), (1,)), ((), ())), preferred_element_type=jnp.float32
                 )
@@ -299,8 +316,8 @@
     mixed = mixed[:QUAD]
     real = jnp.where(prow <= pcol, mixed, flipped)
     imag = jnp.where(prow > pcol, mixed, jnp.where(prow == pcol, 0.0, -flipped))
-    gram_ref[0, 0] = real[:ORDER, :ORDER]
-    gram_ref[0, 1] = imag[:ORDER, :ORDER]
+    gram_ref[0, :, 0] = real[:ORDER, :ORDER]
+    gram_ref[0, :, 1] = imag[:ORDER, :ORDER]
 
     for c in range(nchunk):
         own_spec_copy(c).wait()
@@ -350,8 +367,8 @@
         spec, gram = pl.pallas_call(
             functools.partial(kernel, n, ns, nfreq, nchunk, slab_cells * ns),
             out_shape=(
-                jax.ShapeDtypeStruct((OWN_ROWS, slab_cells), jnp.bfloat16),
-                jax.ShapeDtypeStruct((1, 2, ORDER, ORDER), jnp.float32),
+                jax.ShapeDtypeStruct((NBLK, 2, slab_cells), jnp.bfloat16),
+                jax.ShapeDtypeStruct((1, ORDER, 2, ORDER), jnp.float32),
             ),
             in_specs=[smem, smem, smem, pl.BlockSpec(memory_space=pl.ANY)],
             out_specs=(
@@ -362,7 +379,8 @@
                 pltpu.VMEM((table_rows, nt), jnp.bfloat16),
                 pltpu.VMEM((FREQ_ROWS, nt), jnp.float32),
                 pltpu.VMEM((FREQ_ROWS, nt), jnp.int32),
-                pltpu.VMEM((nchunk, nfreq, OWN_ROWS, width), jnp.bfloat16),
+                pltpu.VMEM((nchunk, nfreq, NBLK, 2, width), jnp.bfloat16),
+                pltpu.VMEM((nchunk, n, rows, width), jnp.bfloat16),
                 pltpu.VMEM((nfreq, GRAM_ROWS, GRAM_ROWS), jnp.float32),
                 pltpu.VMEM((nfreq, QUAD // 2, 128), jnp.bfloat16),
                 pltpu.VMEM((n, QUAD // 2, 128), jnp.bfloat16),
@@ -376,6 +394,7 @@
                 dma((ns,)),
                 dma((ns,)),
                 dma((2, nchunk)),
+                dma((nchunk, n)),
             ]
             + [pltpu.VMEM((nt, width), jnp.bfloat16)] * nchunk,
             compiler_params=pltpu.CompilerParams(
@@ -383,8 +402,8 @@
             ),
             cost_estimate=cost,
         )(starts, freqs, alpha, series)
-        own = spec.reshape(2, OWN_ROWS // 2, slab_cells)[:, :NBLK]
-        return own[None], gram
+        own = jnp.transpose(spec, (1, 0, 2))
+        return own[None], jnp.transpose(gram, (0, 2, 1, 3))
 
     placed = (P("freq", "space"), P(), P(), P())
     return jax.shard_map(

time: 126 us -> 125 us (level)
  no operation moved by 1% of the time
where the time goes in v5:
time: 125 us
  Pallas kernels  120 us (96%)
  local copies, waits for them, and re-layouts  3.57 us (3%)
  between operations  1.29 us (1%)
    pallas_call x1, Pallas kernels, per_device(): pl.pallas_call(functools.partial(kernel, n, ns, nfreq, nchunk, slab_cells...  120 us
    unnamed x2, local copies, waits for them, and re-layouts  3.57 us

profile of v5, /device:TPU:0, one launch (start us, length us, event | category | flops | bytes accessed | tf_op | source)
XLA Modules:
  0.0 125.2 jit_solution(1332876376752375519)
XLA Ops:
  1.3 120.3 %shard_map.59 = (bf16[7,2,16384]{2,1,0:T(2,128)(2,1)}, f32[1,63,2,63]{3,2,1,0:T(2,128)}) custom-call(s32[7]{0:T(128)} %starts_ref.1, s32[16]{0:T(128)} %freqs_ref.1, s32[1]{0:T(128)S(6)} %copy.8.alpha_ref, bf16[128,16384]{1,0:T(8,128)(2,1)} %series_ref.1), custom_call_target="tpu_custom_call" | custom-call | flops 9663676416 | bytes 8388608 | tf_op jit(solution)/shard_map/pallas_call | solution.py:367
  121.6 2.1 %copy.9 = bf16[1,2,7,16384]{3,1,2,0:T(2,128)(2,1)} copy(bf16[1,2,7,16384]{3,1,2,0:T(2,128)(2,1)} %bitcast.4) | data formatting | bytes 917504
  123.7 1.5 %copy.10 = f32[1,2,63,63]{3,1,2,0:T(2,128)} copy(f32[1,2,63,63]{3,1,2,0:T(2,128)} %bitcast.5) | data formatting | bytes 63504

commit v6 on v5

--- a/solution.py
+++ b/solution.py
@@ -66,7 +66,6 @@
     gram_ref,
     table,
     weight,
-    elapsed,
     stage,
     outgoing,
     accum,
@@ -218,20 +217,27 @@
         t = lane + i * 128 - first
         inside = (t >= 0) & (t < NFFT) & used
         window = scale + scale * negative_cosine(t)
-        elapsed[:, cols] = t
         weight[:, cols] = jnp.where(inside, -window, 0.0)
 
     @pl.loop(0, nfreq)
     def _(j):
         bins = freqs_ref[j] + (shift - HALF) * alpha_ref[0]
         base = pl.multiple_of(j * FREQ_ROWS, 16)
-
-        @pl.loop(0, nt // 128)
-        def _(i):
+        turn = bins & 3
+        even = jnp.where(turn == 0, 1.0, jnp.where(turn == 2, -1.0, 0.0))
+        odd = jnp.where(turn == 1, 1.0, jnp.where(turn == 3, -1.0, 0.0))
+        step = bins * (lane - first) + quarter
+        here = negative_cosine(step)
+        ahead = negative_cosine(step + NFFT // 4)
+
+        def column(i, carry):
+            here, ahead = carry
             cols = pl.ds(pl.multiple_of(i * 128, 128), 128)
-            step = bins * elapsed[:, cols] + quarter
-            value = negative_cosine(step) * weight[:, cols]
+            value = here * weight[:, cols]
             table[pl.ds(base, FREQ_ROWS), cols] = value.astype(jnp.bfloat16)
+            return here * even + ahead * odd, ahead * even - here * odd
+
+        lax.fori_loop(0, nt // 128, column, (here, ahead))
 
     for c in range(nchunk):
         own_copy(c).wait()
@@ -345,6 +351,17 @@
         space_copy(lax.rem(my_space + k, ns), my_space).wait_send()
 
 
+def hand_over(spec_in, gram_in, spec_out, gram_out, sems):
+    copies = [
+        pltpu.make_async_copy(spec_in, spec_out, sems.at[0]),
+        pltpu.make_async_copy(gram_in, gram_out, sems.at[1]),
+    ]
+    for copy in copies:
+        copy.start()
+    for copy in copies:
+        copy.wait()
+
+
 def solution(mesh):
     n = mesh.shape["freq"]
     ns = mesh.shape["space"]
@@ -378,7 +395,6 @@
             scratch_shapes=[
                 pltpu.VMEM((table_rows, nt), jnp.bfloat16),
                 pltpu.VMEM((FREQ_ROWS, nt), jnp.float32),
-                pltpu.VMEM((FREQ_ROWS, nt), jnp.int32),
                 pltpu.VMEM((nchunk, nfreq, NBLK, 2, width), jnp.bfloat16),
                 pltpu.VMEM((nchunk, n, rows, width), jnp.bfloat16),
                 pltpu.VMEM((nfreq, GRAM_ROWS, GRAM_ROWS), jnp.float32),
@@ -402,6 +418,18 @@
             ),
             cost_estimate=cost,
         )(starts, freqs, alpha, series)
+        anywhere = pl.BlockSpec(memory_space=pl.ANY)
+        spec, gram = pl.pallas_call(
+            hand_over,
+            out_shape=(
+                jax.ShapeDtypeStruct(spec.shape, spec.dtype),
+                jax.ShapeDtypeStruct(gram.shape, gram.dtype),
+            ),
+            in_specs=[anywhere, anywhere],
+            out_specs=(anywhere, anywhere),
+            scratch_shapes=[dma((2,))],
+            compiler_params=pltpu.CompilerParams(vmem_limit_bytes=60 * 1024 * 1024),
+        )(spec, gram)
         own = jnp.transpose(spec, (1, 0, 2))
         return own[None], jnp.transpose(gram, (0, 2, 1, 3))
 

time: 125 us -> 139 us (1.11)
  Pallas kernels: 120 us -> 137 us
  local copies, waits for them, and re-layouts: 3.57 us -> 0 us
    pallas_call x0 -> x1, Pallas kernels: none -> 17 us  [per_device(): pl.pallas_call(hand_over, out_shape=(jax.ShapeDtypeStruct(spec.shape, spe...]
    unnamed x2 -> x0, local copies, waits for them, and re-layouts: 3.57 us -> none
where the time goes in v6:
time: 139 us
  Pallas kernels  137 us (99%)
    pallas_call x1, Pallas kernels, per_device(): pl.pallas_call(functools.partial(kernel, n, ns, nfreq, nchunk, slab_cells...  120 us
    pallas_call x1, Pallas kernels, per_device(): pl.pallas_call(hand_over, out_shape=(jax.ShapeDtypeStruct(spec.shape, spe...  17 us

profile of v6, /device:TPU:0, one launch (start us, length us, event | category | flops | bytes accessed | tf_op | source)
XLA Modules:
  0.0 138.6 jit_solution(4192459520942175331)
XLA Ops:
  1.3 120.3 %shard_map.59 = (bf16[7,2,16384]{2,1,0:T(2,128)(2,1)}, f32[1,63,2,63]{3,2,1,0:T(2,128)}) custom-call(s32[7]{0:T(128)} %starts_ref.1, s32[16]{0:T(128)} %freqs_ref.1, s32[1]{0:T(128)S(6)} %copy.6.alpha_ref, bf16[128,16384]{1,0:T(8,128)(2,1)} %series_ref.1), custom_call_target="tpu_custom_call" | custom-call | flops 9663676416 | bytes 8388608 | tf_op jit(solution)/shard_map/pallas_call | solution.py:384
  121.6 17.0 %shard_map.60 = (bf16[7,2,16384]{2,1,0:T(2,128)(2,1)}, f32[1,63,2,63]{3,2,1,0:T(2,128)}) custom-call(bf16[7,2,16384]{2,1,0:T(2,128)(2,1)} %get-tuple-element.6.spec_in, f32[1,63,2,63]{3,2,1,0:T(2,128)} %get-tuple-element.7.gram_in), custom_call_target="tpu_custom_call" | custom-call | tf_op jit(solution)/shard_map/pallas_call | solution.py:422

commit v7 on v5

--- a/solution.py
+++ b/solution.py
@@ -18,6 +18,7 @@
 OWN_ROWS = 16
 FREQ_ROWS = GRAM_ROWS + OWN_ROWS
 GROUP = 4
+PARTS = 4
 MESH = pl.DeviceIdType.MESH
 
 
@@ -66,9 +67,9 @@
     gram_ref,
     table,
     weight,
-    elapsed,
     stage,
     outgoing,
+    sums,
     accum,
     pack_out,
     pack_in,
@@ -218,22 +219,59 @@
         t = lane + i * 128 - first
         inside = (t >= 0) & (t < NFFT) & used
         window = scale + scale * negative_cosine(t)
-        elapsed[:, cols] = t
         weight[:, cols] = jnp.where(inside, -window, 0.0)
 
     @pl.loop(0, nfreq)
     def _(j):
         bins = freqs_ref[j] + (shift - HALF) * alpha_ref[0]
         base = pl.multiple_of(j * FREQ_ROWS, 16)
-
-        @pl.loop(0, nt // 128)
-        def _(i):
+        turn = bins & 3
+        even = jnp.where(turn == 0, 1.0, jnp.where(turn == 2, -1.0, 0.0))
+        odd = jnp.where(turn == 1, 1.0, jnp.where(turn == 3, -1.0, 0.0))
+        step = bins * (lane - first) + quarter
+        here = negative_cosine(step)
+        ahead = negative_cosine(step + NFFT // 4)
+
+        def column(i, carry):
+            here, ahead = carry
             cols = pl.ds(pl.multiple_of(i * 128, 128), 128)
-            step = bins * elapsed[:, cols] + quarter
-            value = negative_cosine(step) * weight[:, cols]
+            value = here * weight[:, cols]
             table[pl.ds(base, FREQ_ROWS), cols] = value.astype(jnp.bfloat16)
-
-    for c in range(nchunk):
+            return here * even + ahead * odd, ahead * even - here * odd
+
+        lax.fori_loop(0, nt // 128, column, (here, ahead))
+
+    def far_first(step, count):
+        return lax.rem(step + lax.div(me * count, n) + count // 2, count)
+
+    def table_rows(g):
+        return pl.ds(pl.multiple_of(g * (GROUP * FREQ_ROWS), 16), GROUP * FREQ_ROWS)
+
+    def correlate(c, g, result):
+        result = result.astype(jnp.bfloat16)
+        for i in range(GROUP):
+            j = g * GROUP + i
+            lines = result[i * FREQ_ROWS : i * FREQ_ROWS + GRAM_ROWS]
+            own = i * FREQ_ROWS + GRAM_ROWS
+            stage[c, j] = result[own : own + 2 * NBLK].reshape(NBLK, 2, width)
+            product = lax.dot_general(
+                lines, lines, (((1,), (1,)), ((), ())), preferred_element_type=jnp.float32
+            )
+            if c > 0:
+                product += accum[j]
+            if c == nchunk - 1:
+                pack_out[j] = packed(product)
+            else:
+                accum[j] = product
+
+    def send_spectra(c):
+        @pl.loop(0, n - 1)
+        def _(k):
+            spec_copy(c, peer_at(k), me).start()
+
+        own_spec_copy(c).start()
+
+    for c in range(nchunk - 1):
         own_copy(c).wait()
 
         @pl.loop(1, n)
@@ -241,41 +279,54 @@
             peer = lax.rem(me + k, n)
             raw_copy(c, peer, peer).wait_recv()
 
-        last = c == nchunk - 1
+        @pl.loop(0, groups)
+        def _(g):
+            result = jnp.dot(
+                table[table_rows(g), :], slabs[c][...], preferred_element_type=jnp.float32
+            )
+            correlate(c, g, result)
+
+        send_spectra(c)
+
+    c = nchunk - 1
+    sources = n // PARTS
+    for q in range(PARTS):
+        part_index = far_first(q, PARTS)
+
+        @pl.loop(0, sources)
+        def _(i):
+            peer = part_index * sources + i
+
+            @pl.when(peer != me)
+            def _():
+                raw_copy(c, peer, peer).wait_recv()
+
+            @pl.when(peer == me)
+            def _():
+                own_copy(c).wait()
+
+        span = pl.ds(pl.multiple_of(part_index * (nt // PARTS), 128), nt // PARTS)
 
         @pl.loop(0, groups)
         def _(step):
-            g = lax.rem(step + lax.div(me, GROUP) + groups // 2, groups)
-            base = pl.multiple_of(g * (GROUP * FREQ_ROWS), 16)
+            g = far_first(step, groups)
             result = jnp.dot(
-                table[pl.ds(base, GROUP * FREQ_ROWS), :],
-                slabs[c][...],
-                preferred_element_type=jnp.float32,
-            ).astype(jnp.bfloat16)
-            for i in range(GROUP):
-                j = g * GROUP + i
-                lines = result[i * FREQ_ROWS : i * FREQ_ROWS + GRAM_ROWS]
-                first = i * FREQ_ROWS + GRAM_ROWS
-                stage[c, j] = result[first : first + 2 * NBLK].reshape(NBLK, 2, width)
-                product = lax.dot_general(
-                    lines, lines, (((1,), (1,)), ((), ())), preferred_element_type=jnp.float32
-                )
-                if c > 0:
-                    product += accum[j]
-                if last:
-                    pack_out[j] = packed(product)
-                else:
-                    accum[j] = product
-            for i in range(GROUP):
-                j = g * GROUP + i
-
-                @pl.when(j != me)
-                def _():
-                    if last:
+                table[table_rows(g), span], slabs[c][span, :], preferred_element_type=jnp.float32
+            )
+            if q > 0:
+                result += sums[table_rows(g), :]
+            if q < PARTS - 1:
+                sums[table_rows(g), :] = result
+            else:
+                correlate(c, g, result)
+                for i in range(GROUP):
+                    j = g * GROUP + i
+
+                    @pl.when(j != me)
+                    def _():
                         gram_copy(j, me).start()
-                    spec_copy(c, j, me).start()
-
-        own_spec_copy(c).start()
+
+    send_spectra(c)
 
     pack_in[me] = pack_out[me]
 
@@ -378,9 +429,9 @@
             scratch_shapes=[
                 pltpu.VMEM((table_rows, nt), jnp.bfloat16),
                 pltpu.VMEM((FREQ_ROWS, nt), jnp.float32),
-                pltpu.VMEM((FREQ_ROWS, nt), jnp.int32),
                 pltpu.VMEM((nchunk, nfreq, NBLK, 2, width), jnp.bfloat16),
                 pltpu.VMEM((nchunk, n, rows, width), jnp.bfloat16),
+                pltpu.VMEM((table_rows, width), jnp.float32),
                 pltpu.VMEM((nfreq, GRAM_ROWS, GRAM_ROWS), jnp.float32),
                 pltpu.VMEM((nfreq, QUAD // 2, 128), jnp.bfloat16),
                 pltpu.VMEM((n, QUAD // 2, 128), jnp.bfloat16),

time: 125 us -> 127 us (1.016)
  Pallas kernels: 120 us -> 122 us
    pallas_call x1, Pallas kernels: 120 us -> 122 us  [per_device(): pl.pallas_call(functools.partial(kernel, n, ns, nfreq, nchunk, slab_cells...]
where the time goes in v7:
time: 127 us
  Pallas kernels  122 us (96%)
  local copies, waits for them, and re-layouts  3.57 us (3%)
  between operations  1.29 us (1%)
    pallas_call x1, Pallas kernels, per_device(): pl.pallas_call(functools.partial(kernel, n, ns, nfreq, nchunk, slab_cells...  122 us
    unnamed x2, local copies, waits for them, and re-layouts  3.57 us

profile of v7, /device:TPU:0, one launch (start us, length us, event | category | flops | bytes accessed | tf_op | source)
XLA Modules:
  0.0 126.5 jit_solution(10638411851726821135)
XLA Ops:
  1.3 121.7 %shard_map.59 = (bf16[7,2,16384]{2,1,0:T(2,128)(2,1)}, f32[1,63,2,63]{3,2,1,0:T(2,128)}) custom-call(s32[7]{0:T(128)} %starts_ref.1, s32[16]{0:T(128)} %freqs_ref.1, s32[1]{0:T(128)S(6)} %copy.8.alpha_ref, bf16[128,16384]{1,0:T(8,128)(2,1)} %series_ref.1), custom_call_target="tpu_custom_call" | custom-call | flops 9663676416 | bytes 8388608 | tf_op jit(solution)/shard_map/pallas_call | solution.py:418
  123.0 2.1 %copy.9 = bf16[1,2,7,16384]{3,1,2,0:T(2,128)(2,1)} copy(bf16[1,2,7,16384]{3,1,2,0:T(2,128)(2,1)} %bitcast.4) | data formatting | bytes 917504
  125.1 1.5 %copy.10 = f32[1,2,63,63]{3,1,2,0:T(2,128)} copy(f32[1,2,63,63]{3,1,2,0:T(2,128)} %bitcast.5) | data formatting | bytes 63504

commit v8 on v7

--- a/solution.py
+++ b/solution.py
@@ -405,7 +405,7 @@
         nfreq = freqs.shape[0]
         nt = rows * n
         own_cells = slab_cells // n
-        nchunk = max(2, own_cells // 256)
+        nchunk = max(2, own_cells // 512)
         width = own_cells // nchunk
         smem = pl.BlockSpec(memory_space=pltpu.SMEM)
         table_rows = nfreq * FREQ_ROWS

time: 127 us -> 126 us (level)
  no operation moved by 1% of the time
where the time goes in v8:
time: 126 us
  Pallas kernels  121 us (96%)
  local copies, waits for them, and re-layouts  3.57 us (3%)
  between operations  1.29 us (1%)
    pallas_call x1, Pallas kernels, per_device(): pl.pallas_call(functools.partial(kernel, n, ns, nfreq, nchunk, slab_cells...  121 us
    unnamed x2, local copies, waits for them, and re-layouts  3.57 us

profile of v8, /device:TPU:0, one launch (start us, length us, event | category | flops | bytes accessed | tf_op | source)
XLA Modules:
  0.0 125.7 jit_solution(8813271163585885043)
XLA Ops:
  1.3 120.9 %shard_map.59 = (bf16[7,2,16384]{2,1,0:T(2,128)(2,1)}, f32[1,63,2,63]{3,2,1,0:T(2,128)}) custom-call(s32[7]{0:T(128)} %starts_ref.1, s32[16]{0:T(128)} %freqs_ref.1, s32[1]{0:T(128)S(6)} %copy.8.alpha_ref, bf16[128,16384]{1,0:T(8,128)(2,1)} %series_ref.1), custom_call_target="tpu_custom_call" | custom-call | flops 9663676416 | bytes 8388608 | tf_op jit(solution)/shard_map/pallas_call | solution.py:418
  122.2 2.1 %copy.9 = bf16[1,2,7,16384]{3,1,2,0:T(2,128)(2,1)} copy(bf16[1,2,7,16384]{3,1,2,0:T(2,128)(2,1)} %bitcast.4) | data formatting | bytes 917504
  124.3 1.5 %copy.10 = f32[1,2,63,63]{3,1,2,0:T(2,128)} copy(f32[1,2,63,63]{3,1,2,0:T(2,128)} %bitcast.5) | data formatting | bytes 63504

commit v9 on v7

--- a/solution.py
+++ b/solution.py
@@ -105,8 +105,13 @@
             series_ref.at[:, cells], outgoing.at[c, peer], stage_sem.at[c, peer]
         )
 
+    half = n // 2
+    place = lax.rem(me, half)
+
     def peer_at(k):
-        return lax.rem(me + 1 + lax.rem(k + n // 2 - 1, n - 1), n)
+        far = half - (me - place) + lax.rem(place + lax.div(k, 2), half)
+        near = me - place + lax.rem(place + 1 + lax.div(k, 2), half)
+        return far + lax.rem(k, 2) * (near - far)
 
     barrier = pltpu.get_barrier_semaphore()
 

time: 127 us -> 127 us (level)
  no operation moved by 1% of the time
where the time goes in v9:
time: 127 us; the launch traced here: 126 us
  Pallas kernels  122 us (96%)
  local copies, waits for them, and re-layouts  3.57 us (3%)
  between operations  1.29 us (1%)
    pallas_call x1, Pallas kernels, per_device(): pl.pallas_call(functools.partial(kernel, n, ns, nfreq, nchunk, slab_cells...  122 us
    unnamed x2, local copies, waits for them, and re-layouts  3.57 us

profile of v9, /device:TPU:0, one launch (start us, length us, event | category | flops | bytes accessed | tf_op | source)
XLA Modules:
  0.0 126.5 jit_solution(6647628295632687435)
XLA Ops:
  1.3 121.6 %shard_map.59 = (bf16[7,2,16384]{2,1,0:T(2,128)(2,1)}, f32[1,63,2,63]{3,2,1,0:T(2,128)}) custom-call(s32[7]{0:T(128)} %starts_ref.1, s32[16]{0:T(128)} %freqs_ref.1, s32[1]{0:T(128)S(6)} %copy.8.alpha_ref, bf16[128,16384]{1,0:T(8,128)(2,1)} %series_ref.1), custom_call_target="tpu_custom_call" | custom-call | flops 9663676416 | bytes 8388608 | tf_op jit(solution)/shard_map/pallas_call | solution.py:423
  122.9 2.1 %copy.9 = bf16[1,2,7,16384]{3,1,2,0:T(2,128)(2,1)} copy(bf16[1,2,7,16384]{3,1,2,0:T(2,128)(2,1)} %bitcast.4) | data formatting | bytes 917504
  125.0 1.5 %copy.10 = f32[1,2,63,63]{3,1,2,0:T(2,128)} copy(f32[1,2,63,63]{3,1,2,0:T(2,128)} %bitcast.5) | data formatting | bytes 63504
